TPU v7x, 32 devices: a whole 2x2x4 slice. The times are simulated.
32 devices in a mesh: tensor: 4 (over y, x), request: 8 (over z, core).
Axes of the slice: x: 2, y: 2, z: 4, core: 2. Of those that a mesh axis runs over, the one named last changes fastest.
Arguments:
- hidden: bfloat16 [64, 2048], P('request'), may hold values from -6 to 6
- norm_gain: float32 [2048], replicated, may hold values from 0.1 to 1.9
- w_query: bfloat16 [2048, 2048], P(None, 'tensor'), may hold values from -0.125 to 0.125
- w_keyval: bfloat16 [2048, 512], P(None, 'tensor'), may hold values from -0.125 to 0.125
- w_output: bfloat16 [2048, 2048], P('tensor'), may hold values from -0.125 to 0.125
- node_cache: bfloat16 [8, 4, 512, 128], P('request', 'tensor'), may hold values from -300 to 300
- leaf_cache: bfloat16 [64, 4, 128, 128], P('request', 'tensor'), may hold values from -300 to 300
- leaf_branch: int32 [64], replicated, may hold values from 0 to 3
- branch_root: int32 [4], replicated, may hold values from 0 to 1
- root_owner: int32 [2], replicated, may hold values from 0 to 7, as said below
- branch_owner: int32 [4], replicated, may hold values from 1 to 6, as said below
- root_len: int32 [2], replicated, may hold values from 1 to 512, as said below
- branch_len: int32 [4], replicated, may hold values from 1 to 512, as said below
- leaf_len: int32 [64], P('request'), may hold values from 0 to 127, as said below
Outputs:
- mixed: bfloat16 [64, 2048], P('request', 'tensor')
- new_entries: bfloat16 [64, 4, 128], P('request', 'tensor')
Inputs may be any that keep to these rules, and one draw needn't show every extreme that they name: The 2 entries of root_owner are all different slots. `branch_owner`: different from every entry of root_owner and from one another. `root_len`: some root has exactly 512 positions. `branch_len`: some branch has exactly 512 positions. `leaf_len`: some leaf has exactly 127 positions.
All inputs are finite; a program needn't handle non-finite values.
Results may differ from a plain program's by a relative error of at most 0.029.
Values may be sent and summed in bfloat16 or wider, within the bound.
A program may use at most 128 MiB of HBM per device.

v0:
```python
import jax
import jax.numpy as jnp
from jax import lax
from jax.sharding import PartitionSpec as P

FLOOR = -1e30


def rotate(values_in, positions):
    half_dim = values_in.shape[-1] // 2
    inverse_freq = 10000.0 ** (
        -(jnp.arange(half_dim, dtype=jnp.float32) * 2.0 / values_in.shape[-1])
    )
    angles = positions.astype(jnp.float32)[..., None] * inverse_freq
    angles = jnp.concatenate([angles, angles], -1)
    turned = jnp.concatenate([-values_in[..., half_dim:], values_in[..., :half_dim]], -1)
    return values_in * jnp.cos(angles) + turned * jnp.sin(angles)


def soft_part(scores, usable, value_rows, pattern):
    scores = jnp.where(usable, scores, FLOOR)
    peak = jnp.max(scores, -1)
    weights = jnp.where(usable, jnp.exp(scores - peak[..., None]), 0.0).astype(jnp.bfloat16)
    summed = jnp.einsum(pattern, weights, value_rows, preferred_element_type=jnp.float32)
    weight_sum = jnp.sum(weights.astype(jnp.float32), -1)
    return (summed, weight_sum, peak)


def local(
    hidden,
    norm_gain,
    w_query,
    w_keyval,
    w_output,
    node_cache,
    leaf_cache,
    leaf_branch,
    branch_root,
    root_owner,
    branch_owner,
    root_len,
    branch_len,
    leaf_len,
):
    head_dim = w_keyval.shape[1] // 2
    local_leaves = hidden.shape[0]
    group = w_query.shape[1] // head_dim
    factor = head_dim ** (-0.5)
    device = lax.axis_index("request")
    offset = device * local_leaves
    widened = hidden.astype(jnp.float32)
    normed = (
        widened * lax.rsqrt(jnp.mean(widened * widened, -1, keepdims=True) + 1e-05) * norm_gain
    ).astype(jnp.bfloat16)
    branch_ids = jnp.arange(branch_root.shape[0], dtype=jnp.int32)
    root_ids = jnp.arange(root_owner.shape[0], dtype=jnp.int32)
    branch_hits = leaf_branch[:, None] == branch_ids[None, :]
    leaf_root = jnp.sum(jnp.where(branch_hits, branch_root[None, :], 0), 1)
    root_hits = leaf_root[:, None] == root_ids[None, :]
    prefix_all = jnp.sum(jnp.where(root_hits, root_len[None, :], 0), 1) + jnp.sum(
        jnp.where(branch_hits, branch_len[None, :], 0), 1
    )
    positions = lax.dynamic_slice_in_dim(prefix_all, offset, local_leaves) + leaf_len
    raw_query = jnp.dot(normed, w_query, preferred_element_type=jnp.float32).reshape(
        local_leaves, group, head_dim
    )
    queries = rotate(raw_query, positions[:, None]).astype(jnp.bfloat16)
    raw_entry = jnp.dot(normed, w_keyval, preferred_element_type=jnp.float32)
    new_entry = jnp.concatenate(
        [rotate(raw_entry[:, :head_dim], positions), raw_entry[:, head_dim:]], -1
    ).astype(jnp.bfloat16)
    leaf_rows = leaf_cache[:, 0]
    slot_index = jnp.arange(leaf_rows.shape[1], dtype=jnp.int32)
    appended = jnp.where(
        (slot_index[None, :] == leaf_len[:, None])[:, :, None], new_entry[:, None, :], leaf_rows
    )
    leaf_scores = (
        jnp.einsum(
            "lgd,lkd->lgk", queries, appended[:, :, :head_dim], preferred_element_type=jnp.float32
        )
        * factor
    )
    leaf_usable = (slot_index[None, :] <= leaf_len[:, None])[:, None, :]
    leaf_sum, leaf_weight, leaf_peak = soft_part(
        leaf_scores, leaf_usable, appended[:, :, head_dim:], "lgk,lkd->lgd"
    )
    everyone = lax.all_gather(
        queries.reshape(local_leaves, group * head_dim), "request", axis=0, tiled=True
    )
    total_leaves = everyone.shape[0]
    mine_all = jnp.any(branch_hits & (branch_owner == device)[None, :], 1) | jnp.any(
        root_hits & (root_owner == device)[None, :], 1
    )
    my_length = jnp.sum(jnp.where(root_owner == device, root_len, 0)) + jnp.sum(
        jnp.where(branch_owner == device, branch_len, 0)
    )
    node_rows = node_cache[0, 0]
    node_usable = jnp.arange(node_rows.shape[0], dtype=jnp.int32) < my_length
    block_rows = 128 if total_leaves % 128 == 0 else total_leaves
    block_count = total_leaves // block_rows

    def owner_block(stacked_in):
        rows_query, rows_mine = stacked_in
        scores = (
            jnp.einsum(
                "ngd,kd->ngk",
                rows_query,
                node_rows[:, :head_dim],
                preferred_element_type=jnp.float32,
            )
            * factor
        )
        usable = rows_mine[:, None, None] & node_usable[None, None, :]
        return soft_part(scores, usable, node_rows[:, head_dim:], "ngk,kd->ngd")

    results = lax.map(
        owner_block,
        (
            everyone.reshape(block_count, block_rows, group, head_dim),
            mine_all.reshape(block_count, block_rows),
        ),
    )
    own_sum = results[0].reshape(total_leaves, group, head_dim)
    own_weight = results[1].reshape(total_leaves, group)
    own_peak = results[2].reshape(total_leaves, group)
    global_peak = lax.pmax(own_peak.astype(jnp.bfloat16), "request").astype(own_peak.dtype)
    scaled = jnp.exp(own_peak - global_peak)
    shared_sum, remote_weight = (
        lax.psum_scatter(
            (scaled[..., None] * own_sum).reshape(total_leaves, group * head_dim),
            "request",
            scatter_dimension=0,
            tiled=True,
        ),
        lax.psum_scatter(scaled * own_weight, "request", scatter_dimension=0, tiled=True),
    )
    remote_sum = shared_sum.reshape(local_leaves, group, head_dim)
    remote_peak = lax.dynamic_slice_in_dim(global_peak, offset, local_leaves)
    peak = jnp.maximum(remote_peak, leaf_peak)
    remote_scale = jnp.exp(remote_peak - peak)
    leaf_scale = jnp.exp(leaf_peak - peak)
    numerator = remote_scale[..., None] * remote_sum + leaf_scale[..., None] * leaf_sum
    denominator = remote_scale * remote_weight + leaf_scale * leaf_weight
    attended = (
        (numerator / denominator[..., None])
        .astype(jnp.bfloat16)
        .reshape(local_leaves, group * head_dim)
    )
    term = jnp.dot(attended, w_output, preferred_element_type=jnp.float32)
    mixed = lax.psum_scatter(term, "tensor", scatter_dimension=1, tiled=True).astype(jnp.bfloat16)
    return (mixed, new_entry[:, None, :])


def solution(mesh):
    in_specs = (
        P("request", None),
        P(),
        P(None, "tensor"),
        P(None, "tensor"),
        P("tensor", None),
        P("request", "tensor", None, None),
        P("request", "tensor", None, None),
        P(),
        P(),
        P(),
        P(),
        P(),
        P(),
        P("request"),
    )
    out_specs = (P("request", "tensor"), P("request", "tensor", None))
    return jax.shard_map(local, mesh=mesh, in_specs=in_specs, out_specs=out_specs, check_vma=False)
```

profile of v0, /device:TPU:0, one launch (start us, length us, event | category | flops | bytes accessed | tf_op | source)
XLA Modules:
  0.0 129.2 jit_solution(8122106469692262042)
XLA Ops:
  7.3 0.0 reduce-scatter.3.cloned.1.call-start
  7.3 1.1 fusion.7
  8.4 1.3 %fusion.11 = f32[8,128]{1,0:T(8,128)S(1)} fusion(bf16[2048,128]{1,0:T(8,128)(2,1)} %param.17, bf16[8,2048]{1,0:T(8,128)(2,1)} %param.14, f32[2048]{0:T(1024)} %param.15, f32[8]{0:T(128)S(1)} %add_rsqrt_fusion), kind=kOutput, calls=%fused_computation.32 | convolution fusion | flops 4259840 | bytes 569376 | tf_op jit(solution)/shard_map/dot_general | solution.py:68
  9.7 2.1 %fusion.13 = f32[8,512]{1,0:T(8,128)S(1)} fusion(bf16[2048,512]{1,0:T(8,128)(2,1)} %param.16, bf16[8,2048]{1,0:T(8,128)(2,1)} %param.14, f32[2048]{0:T(1024)} %param.15, f32[8]{0:T(128)S(1)} %add_rsqrt_fusion), kind=kOutput, calls=%fused_computation.33 | convolution fusion | flops 16842752 | bytes 2154528 | tf_op jit(solution)/shard_map/dot_general | solution.py:64
  11.8 0.1 reshape.264
  11.8 0.1 slice_negate_fusion
  12.0 0.1 select_reduce_fusion
  12.0 0.1 select_reduce_fusion.2
  12.1 0.1 add_convert_fusion.3
  12.2 0.1 slice_negate_fusion.1
  12.3 0.7 fusion.21
  13.0 0.1 maximum_multiply_fusion
  13.1 0.1 mul.149
  13.2 0.1 mul.145
  13.2 0.3 copy-done.5
  13.6 15.6 %all_gather.3 = bf16[64,512]{1,0:T(8,128)(2,1)S(1)} all-gather(bf16[8,512]{1,0:T(8,128)(2,1)S(1)} %add_convert_fusion.2), channel_id=1, replica_groups=mesh['tensor'=4,'request'=8] {'request'}, dimensions={0}, use_global_device_ids=true | all-gather | bytes 73728 | tf_op jit(solution)/shard_map/all_gather | solution.py:87
  29.2 0.1 squeeze.14
  29.4 0.7 select_reduce_fusion.4
  30.1 0.1 and_reduce_fusion
  30.2 0.6 select_reduce_fusion.3
  30.8 0.1 fusion.23
  32.2 0.1 copy.20
  32.3 0.1 broadcast_and_fusion
  32.4 0.4 fusion.28
  32.8 0.4 convert_reduce_fusion
  33.2 29.1 %pmax.7 = bf16[64,8]{1,0:T(8,128)(2,1)S(1)} all-reduce(bf16[64,8]{1,0:T(8,128)(2,1)S(1)} %convert_element_type.56), channel_id=1, replica_groups=mesh['tensor'=4,'request'=8] {'request'}, use_global_device_ids=true, to_apply=%region_9.10 | all-reduce | flops 512 | bytes 2048 | tf_op jit(solution)/shard_map/pmax | solution.py:126
  62.3 0.6 fusion.27
  62.9 1.1 convolution_multiply_fusion.1
  64.0 1.7 %mul.159 = f32[64,512]{1,0:T(8,128)} reshape(f32[64,8,64]{2,1,0:T(8,128)} %convolution_multiply_fusion.1) | data formatting | bytes 262144 | tf_op jit(solution)/shard_map/mul | solution.py:130
  65.7 0.0 reduce-scatter.5.cloned.1.call-start
  65.8 0.1 slice.62
  65.9 0.1 iota_compare_fusion.1
  65.9 1.1 copy.21
  67.1 0.1 pad_maximum_fusion.1
  67.2 0.2 bitcast_select_fusion
  67.4 0.9 fusion.29
  68.3 0.2 convert_reduce_fusion.1
  68.5 1.2 dynamic-slice.1
  70.3 26.5 %all-reduce = f32[64,8]{1,0:T(8,128)S(1)} all-reduce(f32[64,8]{1,0:T(8,128)} %get-tuple-element.23), channel_id=3, replica_groups=mesh['tensor'=4,'request'=8] {'request'}, use_global_device_ids=true, to_apply=%region_13.14.clone | all-reduce | flops 512 | bytes 4096
  96.8 0.0 reduce-scatter.3.cloned.1.call-done
  96.8 0.8 reshape.265
  97.6 0.2 fusion.4
  97.9 0.1 reshape.266
  98.0 1.0 fusion.30
  99.0 0.1 slice_bitcast_fusion.4
  99.1 0.7 pad_maximum_fusion.2
  99.7 21.3 %reduce-scatter.5.cloned.1.call-done = f32[8,512]{1,0:T(8,128)} async-done(((f32[8,2048]{1,0:T(8,128)}), f32[8,512]{1,0:T(8,128)}) %reduce-scatter.5.cloned.1.call-update) | async-done | bytes 16400 | tf_op jit(solution)/shard_map/reduce_scatter | solution.py:150
  121.1 1.3 %convert_element_type.64 = bf16[8,512]{1,0:T(8,128)(2,1)} convert(f32[8,512]{1,0:T(8,128)} %reduce-scatter.5.cloned.1.call-done) | non-fusion elementwise | flops 4096 | bytes 24576 | tf_op jit(solution)/shard_map/convert_element_type | solution.py:150
  (43 shorter events, 0.2 us)
Async XLA Ops:
  7.2 90.8 %copy-start = (bf16[512,2048]{1,0:T(8,128)(2,1)S(1)}, bf16[512,2048]{1,0:T(8,128)(2,1)}, u32[]{:S(2)}) copy-start(bf16[512,2048]{1,0:T(8,128)(2,1)} %param.18) | copy-start | bytes 6291460
  7.2 4.7 %copy-start.15 = (s32[64]{0:T(128)S(1)}, s32[64]{0:T(128)}, u32[]{:S(2)}) copy-start(s32[64]{0:T(128)} %param.21) | copy-start | bytes 772
  7.2 4.7 %copy-start.11 = (s32[4]{0:T(128)S(1)}, s32[4]{0:T(128)}, u32[]{:S(2)}) copy-start(s32[4]{0:T(128)} %param.22) | copy-start | bytes 52
  7.2 4.7 %copy-start.8 = (s32[4]{0:T(128)S(1)}, s32[4]{0:T(128)}, u32[]{:S(2)}) copy-start(s32[4]{0:T(128)} %param.26) | copy-start | bytes 52
  7.2 4.8 %copy-start.12 = (s32[2]{0:T(128)S(1)}, s32[2]{0:T(128)}, u32[]{:S(2)}) copy-start(s32[2]{0:T(128)} %param.25) | copy-start | bytes 28
  7.2 4.9 %copy-start.9 = (s32[8]{0:T(128)S(1)}, s32[8]{0:T(128)}, u32[]{:S(2)}) copy-start(s32[8]{0:T(128)} %param.27) | copy-start | bytes 100
  7.2 22.1 %copy-start.13 = (s32[2]{0:T(128)S(1)}, s32[2]{0:T(128)}, u32[]{:S(2)}) copy-start(s32[2]{0:T(128)} %param.23) | copy-start | bytes 28
  7.2 22.9 %copy-start.14 = (s32[4]{0:T(128)S(1)}, s32[4]{0:T(128)}, u32[]{:S(2)}) copy-start(s32[4]{0:T(128)} %param.24) | copy-start | bytes 52
  7.3 24.9 %copy-start.1 = (bf16[1,1,512,128]{3,2,1,0:T(8,128)(2,1)S(1)}, bf16[1,1,512,128]{3,2,1,0:T(8,128)(2,1)}, u32[]{:S(2)}) copy-start(bf16[1,1,512,128]{3,2,1,0:T(8,128)(2,1)} %param.19) | copy-start | bytes 393220
  7.3 89.5 %reduce-scatter.3.cloned.1.call-start = ((), (), s32[]{:S(2)}) async-start(), calls=%async_computation.2 | async-start | bytes 147456 | tf_op jit(solution)/shard_map/reduce_scatter | solution.py:129
  9.7 3.3 %copy-start.2 = (f32[8,128]{1,0:T(8,128)}, f32[8,128]{1,0:T(8,128)S(1)}, u32[]{:S(2)}) copy-start(f32[8,128]{1,0:T(8,128)S(1)} %fusion.11) | copy-start | bytes 12292
  13.0 0.6 copy-start.5
  32.8 33.0 %copy-start.3 = (f32[8,128]{1,0:T(8,128)S(1)}, f32[8,128]{1,0:T(8,128)}, u32[]{:S(2)}) copy-start(f32[8,128]{1,0:T(8,128)} %copy-done.2) | copy-start | bytes 12292
  32.8 33.1 %copy-start.10 = (s32[8]{0:T(128)S(1)}, s32[8]{0:T(128)}, u32[]{:S(2)}) copy-start(s32[8]{0:T(128)} %param.27) | copy-start | bytes 100
  32.8 34.3 %copy-start.6 = (bf16[8,64]{1,0:T(8,128)(2,1)S(1)}, bf16[8,64]{1,0:T(8,128)(2,1)}, u32[]{:S(2)}) copy-start(bf16[8,64]{1,0:T(8,128)(2,1)} %get-tuple-element.40) | copy-start | bytes 3076
  65.7 55.3 %reduce-scatter.5.cloned.1.call-start = ((), (), s32[]{:S(2)}) async-start(), calls=%async_computation.3 | async-start | bytes 81920 | tf_op jit(solution)/shard_map/reduce_scatter | solution.py:150
  65.9 33.0 %copy-start.4 = (f32[8,128]{1,0:T(8,128)S(1)}, f32[8,128]{1,0:T(8,128)}, u32[]{:S(2)}) copy-start(f32[8,128]{1,0:T(8,128)} %copy-done.2) | copy-start | bytes 12292
  65.9 33.1 %copy-start.7 = (bf16[8,64]{1,0:T(8,128)(2,1)S(1)}, bf16[8,64]{1,0:T(8,128)(2,1)}, u32[]{:S(2)}) copy-start(bf16[8,64]{1,0:T(8,128)(2,1)} %get-tuple-element.40) | copy-start | bytes 3076
Sparse Core Ops, SparseCore 0:
  65.9 28.3 reduce-scatter.2
  99.1 21.9 reduce-scatter.4
where the time goes:
time: 130 us; the launch traced here: 129 us
  blocking collectives  71.2 us (55%)
  waiting for transfers between devices  21.4 us (16%)
  between operations  16.1 us (12%)
  other arithmetic  7.39 us (6%)
  matrix products  6.99 us (5%)
  local copies, waits for them, and re-layouts  6.03 us (5%)
    pmax x1, blocking collectives, local(): lax.pmax(own_peak.astype(jnp.bfloat16), 'request').astype(own_peak.dtype)  29.1 us
    unnamed x1, blocking collectives  26.5 us
    reduce_scatter x1, waiting for transfers between devices, local(): lax.psum_scatter(term, 'tensor', scatter_dimension=1, tiled=True)  21.3 us
    all_gather x1, blocking collectives, local(): lax.all_gather(queries.reshape(local_leaves, group * head_dim), 'request'...  15.6 us
    unnamed x35, local copies, waits for them, and re-layouts  2.92 us
  transfers between devices with their start and end apart: 2, of which 1 were waited for; matrix products, arithmetic and copies ran while one was open for 4% of the time, Pallas kernels for 0%

commit v1 on v0

v1 whole, which is shorter than its diff:
```python
import functools

import jax
import jax.numpy as jnp
import numpy as np
from jax import lax
from jax.experimental import pallas as pl
from jax.experimental.pallas import tpu as pltpu
from jax.sharding import PartitionSpec as P

FLOOR = -1e30
MESH = pl.DeviceIdType.MESH
F32 = jnp.float32
BF16 = jnp.bfloat16
LANES = 128
NT = (((1,), (1,)), ((), ()))
NN = (((1,), (0,)), ((), ()))


def each(low, high, step):
    if high - low <= 8:
        for k in range(low, high):
            step(k)
    else:
        lax.fori_loop(low, high, lambda k, carry: (step(k), carry)[1], 0)


def dot(a, b, dims):
    return lax.dot_general(a, b, dims, preferred_element_type=F32)


def kernel(
    n,
    nt,
    hidden,
    gain,
    freq,
    leaf_branch,
    branch_root,
    root_owner,
    branch_owner,
    root_len,
    branch_len,
    leaf_len,
    w_query,
    w_keyval,
    w_output,
    node_hbm,
    leaf_hbm,
    mixed,
    entry,
    wq,
    wkv,
    wo,
    node,
    leaf,
    q_all,
    part_out,
    part_in,
    term_out,
    term_in,
    load_sem,
    q_send,
    q_recv,
    p_send,
    p_recv,
    t_send,
    t_recv,
):
    me = lax.axis_index("request")
    mine = lax.axis_index("tensor")
    rows, width = hidden.shape
    head_dim = LANES // 2
    chunks = wq.shape[1] // LANES
    body_rows = chunks * rows
    factor = head_dim ** (-0.5)
    splits = 4
    depth = width // splits
    cols = wo.shape[2]

    loads = []

    def load(src, dst):
        copy = pltpu.make_async_copy(src, dst, load_sem.at[len(loads)])
        copy.start()
        loads.append(copy)
        return copy

    q_loads = []
    for s in range(splits):
        part = pl.ds(s * depth, depth)
        q_loads.append(
            (load(w_query.at[part], wq.at[part]), load(w_keyval.at[part], wkv.at[part]))
        )
    node_load = load(node_hbm, node)
    leaf_load = load(leaf_hbm, leaf)
    o_loads = []
    for k in range(nt):
        target = lax.rem(mine + k, nt)
        o_loads.append(
            load(w_output.at[:, pl.ds(pl.multiple_of(target * cols, cols), cols)], wo.at[k])
        )

    barrier = pltpu.get_barrier_semaphore()

    def greet(k):
        pl.semaphore_signal(
            barrier, inc=1, device_id=(mine, lax.rem(me + k, n)), device_id_type=MESH
        )

    each(1, n, greet)
    for k in range(1, nt):
        pl.semaphore_signal(
            barrier, inc=1, device_id=(lax.rem(mine + k, nt), me), device_id_type=MESH
        )

    row8 = lax.broadcasted_iota(jnp.int32, (rows, LANES), 0)
    lane8 = lax.broadcasted_iota(jnp.int32, (rows, LANES), 1)
    low8 = lane8 < head_dim
    position = jnp.zeros((rows, LANES), jnp.int32)
    lengths = jnp.zeros((rows, LANES), jnp.int32)
    root_slot, branch_slot = [], []
    for l in range(rows):
        b = leaf_branch[me * rows + l]
        r = branch_root[b]
        own = leaf_len[l]
        position = jnp.where(row8 == l, root_len[r] + branch_len[b] + own, position)
        lengths = jnp.where(row8 == l, own, lengths)
        root_slot.append(lax.rem(root_owner[r] - me + n, n))
        branch_slot.append(lax.rem(branch_owner[b] - me + n, n))
    my_length = jnp.int32(0)
    for owner, length in ((root_owner, root_len), (branch_owner, branch_len)):
        for j in range(owner.shape[0]):
            my_length = my_length + jnp.where(owner[j] == me, length[j], 0)
    angles = position.astype(F32) * freq[...]
    cosine, sine = jnp.cos(angles), jnp.sin(angles)
    first_half = lax.rem(lane8, head_dim) < head_dim // 2

    def rotate(x):
        up = pltpu.roll(x, LANES - head_dim // 2, 1)
        down = pltpu.roll(x, head_dim // 2, 1)
        return x * cosine + jnp.where(first_half, -up, down) * sine

    widened = hidden[...].astype(F32)
    mean = jnp.sum(widened * widened, -1, keepdims=True) * (1.0 / width)
    normed = (widened * lax.rsqrt(mean + 1e-05) * gain[...]).astype(BF16)
    raw = jnp.zeros((rows, wq.shape[1]), F32)
    raw_entry = jnp.zeros((rows, LANES), F32)
    for s in range(splits):
        for copy in q_loads[s]:
            copy.wait()
        part = slice(s * depth, (s + 1) * depth)
        raw = raw + dot(normed[:, part], wq[part, :], NN)
        raw_entry = raw_entry + dot(normed[:, part], wkv[part, :], NN)
    queries = jnp.concatenate(
        [rotate(raw[:, c * LANES : (c + 1) * LANES]) * factor for c in range(chunks)], 0
    ).astype(BF16)
    q_all[0] = queries

    pl.semaphore_wait(barrier, n - 1 + nt - 1)

    def q_copy(k):
        return pltpu.make_async_remote_copy(
            src_ref=q_all.at[0],
            dst_ref=q_all.at[k],
            send_sem=q_send.at[k],
            recv_sem=q_recv.at[k],
            device_id=(mine, lax.rem(me + k, n)),
            device_id_type=MESH,
        )

    each(1, n, lambda k: q_copy(k).start())

    entry_new = jnp.where(low8, rotate(raw_entry), raw_entry).astype(BF16)
    entry[...] = entry_new
    new32 = entry_new.astype(F32)
    swapped = pltpu.roll(new32, head_dim, 1)
    new_key = jnp.where(low8, new32, swapped)
    new_value = jnp.where(low8, swapped, new32)

    def split_rows(rows_in):
        wide = rows_in.astype(F32)
        turned = pltpu.roll(wide, head_dim, 1)
        low = lax.broadcasted_iota(jnp.int32, wide.shape, 1) < head_dim
        keys = (jnp.where(low, wide, 0.0).astype(BF16), jnp.where(low, 0.0, turned).astype(BF16))
        values = (jnp.where(low, turned, 0.0).astype(BF16), jnp.where(low, 0.0, wide).astype(BF16))
        return keys, values

    node_load.wait()
    node_keys, node_values = split_rows(node[...])

    leaf_load.wait()
    leaf_keys, leaf_values = split_rows(leaf[...])
    per_leaf = leaf.shape[0] // rows
    column = lax.broadcasted_iota(jnp.int32, (rows, leaf.shape[0]), 1)
    start = lax.broadcasted_iota(jnp.int32, (rows, leaf.shape[0]), 0) * per_leaf
    usable = (column >= start) & (column < start + lengths[:, :1])
    q32 = queries.astype(F32)
    leaf_stats = [jnp.zeros((rows, LANES), F32), jnp.zeros((rows, LANES), F32)]
    leaf_sum = []
    leaf_scores = [dot(queries, keys, NT) for keys in leaf_keys]
    leaf_weights = [[], []]
    fresh = []
    for c in range(chunks):
        part = slice(c * rows, (c + 1) * rows)
        product = q32[part] * new_key
        pair = []
        for e in range(2):
            score = jnp.sum(jnp.where(low8 if e == 0 else ~low8, product, 0.0), -1, keepdims=True)
            scores = jnp.where(usable, leaf_scores[e][part], FLOOR)
            peak = jnp.maximum(jnp.max(scores, -1, keepdims=True), score)
            weights = jnp.exp(scores - peak).astype(BF16).astype(F32)
            weight = jnp.exp(score - peak).astype(BF16).astype(F32)
            total = jnp.sum(weights, -1, keepdims=True) + weight
            leaf_weights[e].append(weights)
            pair.append(weight)
            here = lane8 == 2 * c + e
            leaf_stats[0] = jnp.where(here, peak, leaf_stats[0])
            leaf_stats[1] = jnp.where(here, total, leaf_stats[1])
        fresh.append(jnp.where(low8, pair[0], pair[1]) * new_value)
    leaf_sum = jnp.concatenate(fresh, 0)
    for e in range(2):
        leaf_sum = leaf_sum + dot(
            jnp.concatenate(leaf_weights[e], 0).astype(BF16), leaf_values[e], NN
        )

    block = min(n, 8)

    def p_copy(k):
        return pltpu.make_async_remote_copy(
            src_ref=part_out.at[k],
            dst_ref=part_in.at[k],
            send_sem=p_send.at[k],
            recv_sem=p_recv.at[k],
            device_id=(mine, lax.rem(me - k + n, n)),
            device_id_type=MESH,
        )

    held = lax.broadcasted_iota(jnp.int32, (block * body_rows, node.shape[0]), 1) < my_length

    def owner_block(first):
        rows_query = q_all[pl.ds(first, block)].reshape(block * body_rows, LANES)
        summed = None
        peaks, totals = [], []
        for e in range(2):
            scores = jnp.where(held, dot(rows_query, node_keys[e], NT), FLOOR)
            peak = jnp.max(scores, -1, keepdims=True)
            weights = jnp.exp(scores - peak).astype(BF16)
            peaks.append(peak)
            totals.append(jnp.sum(weights.astype(F32), -1, keepdims=True))
            term = dot(weights, node_values[e], NN)
            summed = term if summed is None else summed + term
        for j in range(block):
            stats = jnp.zeros((rows, LANES), F32)
            for c in range(chunks):
                at = j * body_rows + c * rows
                for e in range(2):
                    lane = 2 * c + e
                    stats = jnp.where(lane8 == lane, peaks[e][at : at + rows], stats)
                    stats = jnp.where(lane8 == 2 * chunks + lane, totals[e][at : at + rows], stats)
            high = stats.astype(BF16).astype(F32)
            middle = (stats - high).astype(BF16).astype(F32)
            small = (stats - high) - middle
            part_out[first + j] = jnp.concatenate(
                [
                    summed[j * body_rows : (j + 1) * body_rows],
                    jnp.where(low8, high, pltpu.roll(small, head_dim, 1)),
                    middle,
                ],
                0,
            ).astype(BF16)

    each(1, n, lambda k: q_copy(k).wait_recv())
    for first in range(0, n, block):
        if n == block:
            owner_block(0)
        elif first == 0:
            lax.fori_loop(
                0,
                n // block,
                lambda i, carry: (owner_block(i * block), carry)[1],
                0,
            )
    each(1, n, lambda k: p_copy(k).start())
    part_in[0] = part_out[0]
    each(1, n, lambda k: p_copy(k).wait_recv())

    row_of = lax.rem(lax.broadcasted_iota(jnp.int32, part_in.shape[1:], 0), rows)

    def pick(slots):
        chosen = part_in[slots[0]].astype(F32)
        for l in range(1, rows):
            chosen = jnp.where(row_of == l, part_in[slots[l]].astype(F32), chosen)
        high = chosen[body_rows : body_rows + rows]
        stats = (high + chosen[body_rows + rows :]) + pltpu.roll(high, head_dim, 1)
        return chosen[:body_rows], stats, pltpu.roll(stats, LANES - 2 * chunks, 1)

    parts = [pick(root_slot), pick(branch_slot), (leaf_sum, leaf_stats[0], leaf_stats[1])]
    top = jnp.maximum(jnp.maximum(parts[0][1], parts[1][1]), parts[2][1])
    scales = [jnp.exp(p[1] - top) for p in parts]
    bottom = scales[0] * parts[0][2] + scales[1] * parts[1][2] + scales[2] * parts[2][2]
    scales = [s / bottom for s in scales]
    attended = []
    for c in range(chunks):
        part = slice(c * rows, (c + 1) * rows)
        total = None
        for p, s in zip(parts, scales):
            spread = jnp.where(low8, s[:, 2 * c : 2 * c + 1], s[:, 2 * c + 1 : 2 * c + 2])
            term = spread * p[0][part]
            total = term if total is None else total + term
        attended.append(total)
    attended = jnp.concatenate(attended, 1).astype(BF16)

    def t_copy(k):
        return pltpu.make_async_remote_copy(
            src_ref=term_out.at[k],
            dst_ref=term_in.at[k],
            send_sem=t_send.at[k],
            recv_sem=t_recv.at[k],
            device_id=(lax.rem(mine + k, nt), me),
            device_id_type=MESH,
        )

    out_chunks = cols // LANES
    own_term = None
    for k in [*range(1, nt), 0]:
        o_loads[k].wait()
        term = dot(attended, wo[k], NN)
        if k == 0:
            own_term = term
        else:
            term_out[k] = jnp.concatenate(
                [term[:, c * LANES : (c + 1) * LANES] for c in range(out_chunks)], 0
            ).astype(BF16)
            t_copy(k).start()
    for k in range(1, nt):
        t_copy(k).wait_recv()
    for c in range(out_chunks):
        part = slice(c * LANES, (c + 1) * LANES)
        total = own_term[:, part]
        for k in range(1, nt):
            total = total + term_in[k].astype(F32)[c * rows : (c + 1) * rows]
        mixed[:, part] = total.astype(BF16)

    each(1, n, lambda k: q_copy(k).wait_send())
    each(1, n, lambda k: p_copy(k).wait_send())
    for k in range(1, nt):
        t_copy(k).wait_send()


def local(
    n,
    nt,
    hidden,
    norm_gain,
    w_query,
    w_keyval,
    w_output,
    node_cache,
    leaf_cache,
    leaf_branch,
    branch_root,
    root_owner,
    branch_owner,
    root_len,
    branch_len,
    leaf_len,
):
    rows, width = hidden.shape
    head_dim = w_keyval.shape[1] // 2
    inner = w_query.shape[1]
    cols = w_output.shape[1] // nt
    power = (np.arange(LANES) % (head_dim // 2)) * 2.0 / head_dim
    freq = jnp.asarray((10000.0 ** (-power)).astype(np.float32)[None, :])
    node = node_cache.reshape(-1, LANES)
    leaf = leaf_cache.reshape(-1, LANES)
    body_rows = inner // LANES * rows
    vmem = pl.BlockSpec(memory_space=pltpu.VMEM)
    smem = pl.BlockSpec(memory_space=pltpu.SMEM)
    anywhere = pl.BlockSpec(memory_space=pl.ANY)
    dma = pltpu.SemaphoreType.DMA
    mixed, entry = pl.pallas_call(
        functools.partial(kernel, n, nt),
        out_shape=(
            jax.ShapeDtypeStruct((rows, cols), BF16),
            jax.ShapeDtypeStruct((rows, LANES), BF16),
        ),
        in_specs=[vmem] * 3 + [smem] * 7 + [anywhere] * 5,
        out_specs=(vmem, vmem),
        scratch_shapes=[
            pltpu.VMEM(w_query.shape, BF16),
            pltpu.VMEM(w_keyval.shape, BF16),
            pltpu.VMEM((nt, inner, cols), BF16),
            pltpu.VMEM(node.shape, BF16),
            pltpu.VMEM(leaf.shape, BF16),
            pltpu.VMEM((n, body_rows, LANES), BF16),
            pltpu.VMEM((n, body_rows + 2 * rows, LANES), BF16),
            pltpu.VMEM((n, body_rows + 2 * rows, LANES), BF16),
            pltpu.VMEM((nt, cols // LANES * rows, LANES), BF16),
            pltpu.VMEM((nt, cols // LANES * rows, LANES), BF16),
            dma((8 + 2 + nt,)),
            dma((n,)),
            dma((n,)),
            dma((n,)),
            dma((n,)),
            dma((nt,)),
            dma((nt,)),
        ],
        compiler_params=pltpu.CompilerParams(
            collective_id=0, has_side_effects=True, vmem_limit_bytes=40 * 1024 * 1024
        ),
    )(
        hidden,
        norm_gain[None, :],
        freq,
        leaf_branch,
        branch_root,
        root_owner,
        branch_owner,
        root_len,
        branch_len,
        leaf_len,
        w_query,
        w_keyval,
        w_output,
        node,
        leaf,
    )
    return (mixed, entry[:, None, :])


def solution(mesh):
    in_specs = (
        P("request", None),
        P(),
        P(None, "tensor"),
        P(None, "tensor"),
        P("tensor", None),
        P("request", "tensor", None, None),
        P("request", "tensor", None, None),
        P(),
        P(),
        P(),
        P(),
        P(),
        P(),
        P("request"),
    )
    out_specs = (P("request", "tensor"), P("request", "tensor", None))
    run = functools.partial(local, mesh.shape["request"], mesh.shape["tensor"])
    return jax.shard_map(run, mesh=mesh, in_specs=in_specs, out_specs=out_specs, check_vma=False)
```

time: 130 us -> 36.2 us (0.28)
  blocking collectives: 71.2 us -> 0 us
  waiting for transfers between devices: 21.4 us -> 0 us
  Pallas kernels: 0 us -> 21.1 us
  between operations: 16.1 us -> 0.67 us
  local copies, waits for them, and re-layouts: 6.03 us -> 13.9 us
  other arithmetic: 7.39 us -> 0 us
  matrix products: 6.99 us -> 0 us
    pmax x1 -> x0, blocking collectives: 29.1 us -> none  [local(): lax.pmax(own_peak.astype(jnp.bfloat16), 'request').astype(own_peak.dtype)]
    unnamed x1 -> x0, blocking collectives: 26.5 us -> none
    reduce_scatter x2 -> x0, waiting for transfers between devices: 21.3 us -> none  [the longest x1 21.3 us: local(): lax.psum_scatter(term, 'tensor', scatter_dimension=1, tiled=True)]
    pallas_call x0 -> x1, Pallas kernels: none -> 21.1 us  [local(): pl.pallas_call(functools.partial(kernel, n, nt), out_shape=(jax.ShapeDtyp...]
    all_gather x1 -> x0, blocking collectives: 15.6 us -> none  [local(): lax.all_gather(queries.reshape(local_leaves, group * head_dim), 'request'...]
    unnamed x35 -> x32, local copies, waits for them, and re-layouts: 2.92 us -> 13.9 us
    dot_general x7 -> x0, matrix products: 6.99 us -> none  [the longest x1 2.06 us: local(): jnp.dot(normed, w_query, preferred_element_type=jnp.float32)]
    reduce_sum x7 -> x0, other arithmetic: 3.12 us -> none  [the longest x1 1.06 us: local(): jnp.mean(widened * widened, -1, keepdims=True) + 1e-05]
  transfers between devices with their start and end apart: 2 -> 0, of which waited for: 1 -> 0; matrix products, arithmetic and copies ran while one was open for 4% -> 0% of each run, Pallas kernels for 0% -> 0%
where the time goes in v1:
time: 36.2 us; the launch traced here: 35.7 us
  Pallas kernels  21.1 us (58%)
  local copies, waits for them, and re-layouts  13.9 us (38%)
  between operations  0.67 us (2%)
    pallas_call x1, Pallas kernels, local(): pl.pallas_call(functools.partial(kernel, n, nt), out_shape=(jax.ShapeDtyp...  21.1 us
    unnamed x32, local copies, waits for them, and re-layouts  13.9 us

profile of v1, /device:TPU:0, one launch (start us, length us, event | category | flops | bytes accessed | tf_op | source)
XLA Modules:
  0.0 35.7 jit_solution(710212288157512995)
XLA Ops:
  0.6 0.0 copy-start
  0.6 1.6 %copy-done = bf16[2048,512]{1,0:T(8,128)(2,1)S(1)} copy-done((bf16[2048,512]{1,0:T(8,128)(2,1)S(1)}, bf16[2048,512]{1,0:T(8,128)(2,1)}, u32[]{:S(2)}) %copy-start) | copy-done | bytes 2097176
  2.2 0.0 copy-start.1
  2.2 1.6 %copy-done.1 = bf16[512,2048]{1,0:T(8,128)(2,1)S(1)} copy-done((bf16[512,2048]{1,0:T(8,128)(2,1)S(1)}, bf16[512,2048]{1,0:T(8,128)(2,1)}, u32[]{:S(2)}) %copy-start.1) | copy-done | bytes 2097176
  3.8 0.0 copy-start.2
  3.8 1.0 %copy-done.2 = bf16[2048,128]{1,0:T(8,128)(2,1)S(1)} copy-done((bf16[2048,128]{1,0:T(8,128)(2,1)S(1)}, bf16[2048,128]{1,0:T(8,128)(2,1)}, u32[]{:S(2)}) %copy-start.2) | copy-done | bytes 524312
  4.9 0.0 copy-start.3
  4.9 0.9 %copy-done.3 = bf16[8,1,128,128]{3,2,1,0:T(8,128)(2,1)S(1)} copy-done((bf16[8,1,128,128]{3,2,1,0:T(8,128)(2,1)S(1)}, bf16[8,1,128,128]{3,2,1,0:T(8,128)(2,1)}, u32[]{:S(2)}) %copy-start.3) | copy-done | bytes 262168
  5.8 0.0 copy-start.4
  5.8 0.9 %copy-done.4 = bf16[1,1,512,128]{3,2,1,0:T(8,128)(2,1)S(1)} copy-done((bf16[1,1,512,128]{3,2,1,0:T(8,128)(2,1)S(1)}, bf16[1,1,512,128]{3,2,1,0:T(8,128)(2,1)}, u32[]{:S(2)}) %copy-start.4) | copy-done | bytes 131096
  6.7 0.0 copy-start.5
  6.7 0.8 %copy-done.5 = bf16[8,2048]{1,0:T(8,128)(2,1)S(1)} copy-done((bf16[8,2048]{1,0:T(8,128)(2,1)S(1)}, bf16[8,2048]{1,0:T(8,128)(2,1)}, u32[]{:S(2)}) %copy-start.5) | copy-done | bytes 32792
  7.5 0.0 copy-start.6
  7.5 0.7 %copy-done.6 = f32[2048]{0:T(1024)S(1)} copy-done((f32[2048]{0:T(1024)S(1)}, f32[2048]{0:T(1024)}, u32[]{:S(2)}) %copy-start.6) | copy-done | bytes 8216
  8.2 0.0 copy-start.7
  8.2 0.7 %copy-done.7 = s32[64]{0:T(128)S(1)} copy-done((s32[64]{0:T(128)S(1)}, s32[64]{0:T(128)}, u32[]{:S(2)}) %copy-start.7) | copy-done | bytes 280
  8.8 0.0 copy-start.8
  8.8 0.7 %copy-done.8 = s32[4]{0:T(128)S(1)} copy-done((s32[4]{0:T(128)S(1)}, s32[4]{0:T(128)}, u32[]{:S(2)}) %copy-start.8) | copy-done | bytes 40
  9.5 0.0 copy-start.9
  9.5 0.7 %copy-done.9 = s32[2]{0:T(128)S(1)} copy-done((s32[2]{0:T(128)S(1)}, s32[2]{0:T(128)}, u32[]{:S(2)}) %copy-start.9) | copy-done | bytes 32
  10.1 0.0 copy-start.10
  10.1 0.7 %copy-done.10 = s32[4]{0:T(128)S(1)} copy-done((s32[4]{0:T(128)S(1)}, s32[4]{0:T(128)}, u32[]{:S(2)}) %copy-start.10) | copy-done | bytes 40
  10.8 0.0 copy-start.11
  10.8 0.7 %copy-done.11 = s32[2]{0:T(128)S(1)} copy-done((s32[2]{0:T(128)S(1)}, s32[2]{0:T(128)}, u32[]{:S(2)}) %copy-start.11) | copy-done | bytes 32
  11.5 0.0 copy-start.12
  11.5 0.7 %copy-done.12 = s32[4]{0:T(128)S(1)} copy-done((s32[4]{0:T(128)S(1)}, s32[4]{0:T(128)}, u32[]{:S(2)}) %copy-start.12) | copy-done | bytes 40
  12.1 0.0 copy-start.13
  12.1 0.7 %copy-done.13 = s32[8]{0:T(128)S(1)} copy-done((s32[8]{0:T(128)S(1)}, s32[8]{0:T(128)}, u32[]{:S(2)}) %copy-start.13) | copy-done | bytes 56
  12.8 0.0 copy-start.14
  12.8 0.7 %copy-done.14 = f32[1,128]{1,0:T(1,128)S(1)} copy-done((f32[1,128]{1,0:T(1,128)S(1)}, f32[1,128]{1,0:T(1,128)}, u32[]{:S(2)}) %copy-start.14) | copy-done | bytes 536
  13.4 21.1 %shard_map.158 = (bf16[8,512]{1,0:T(8,128)(2,1)S(1)}, bf16[8,128]{1,0:T(8,128)(2,1)S(1)}) custom-call(bf16[8,2048]{1,0:T(8,128)(2,1)S(1)} %copy-done.5, f32[1,2048]{1,0:T(1,128)S(1)} %bitcast.6, f32[1,128]{1,0:T(1,128)S(1)} %copy-done.14, s32[64]{0:T(128)S(1)} %copy-done.7, s32[4]{0:T(128)S(1)} %copy-done.8, s32[2]{0:T(128)S(1)} %copy-done.9, ...), custom_call_target="tpu_custom_call" | custom-call | tf_op jit(solution)/shard_map/pallas_call | solution.py:382
  34.5 0.6 %copy.19 = bf16[8,512]{1,0:T(8,128)(2,1)} copy(bf16[8,512]{1,0:T(8,128)(2,1)S(1)} %get-tuple-element.8) | data formatting | bytes 16384
  35.1 0.6 %copy.20 = bf16[8,1,128]{2,0,1:T(8,128)(2,1)} copy(bf16[8,1,128]{2,0,1:T(8,128)(2,1)S(1)} %bitcast.7) | data formatting | bytes 4096
Async XLA Ops:
  0.6 1.6 %copy-start = (bf16[2048,512]{1,0:T(8,128)(2,1)S(1)}, bf16[2048,512]{1,0:T(8,128)(2,1)}, u32[]{:S(2)}) copy-start(bf16[2048,512]{1,0:T(8,128)(2,1)} %w_query.1) | copy-start | bytes 6291460
  2.2 1.6 %copy-start.1 = (bf16[512,2048]{1,0:T(8,128)(2,1)S(1)}, bf16[512,2048]{1,0:T(8,128)(2,1)}, u32[]{:S(2)}) copy-start(bf16[512,2048]{1,0:T(8,128)(2,1)} %w_output.1) | copy-start | bytes 6291460
  3.8 1.0 %copy-start.2 = (bf16[2048,128]{1,0:T(8,128)(2,1)S(1)}, bf16[2048,128]{1,0:T(8,128)(2,1)}, u32[]{:S(2)}) copy-start(bf16[2048,128]{1,0:T(8,128)(2,1)} %w_keyval.1) | copy-start | bytes 1572868
  4.9 0.9 %copy-start.3 = (bf16[8,1,128,128]{3,2,1,0:T(8,128)(2,1)S(1)}, bf16[8,1,128,128]{3,2,1,0:T(8,128)(2,1)}, u32[]{:S(2)}) copy-start(bf16[8,1,128,128]{3,2,1,0:T(8,128)(2,1)} %param.21) | copy-start | bytes 786436
  5.8 0.9 %copy-start.4 = (bf16[1,1,512,128]{3,2,1,0:T(8,128)(2,1)S(1)}, bf16[1,1,512,128]{3,2,1,0:T(8,128)(2,1)}, u32[]{:S(2)}) copy-start(bf16[1,1,512,128]{3,2,1,0:T(8,128)(2,1)} %param.20) | copy-start | bytes 393220
  6.7 0.8 %copy-start.5 = (bf16[8,2048]{1,0:T(8,128)(2,1)S(1)}, bf16[8,2048]{1,0:T(8,128)(2,1)}, u32[]{:S(2)}) copy-start(bf16[8,2048]{1,0:T(8,128)(2,1)} %hidden.1) | copy-start | bytes 98308
  7.5 0.7 %copy-start.6 = (f32[2048]{0:T(1024)S(1)}, f32[2048]{0:T(1024)}, u32[]{:S(2)}) copy-start(f32[2048]{0:T(1024)} %param.16) | copy-start | bytes 24580
  8.2 0.7 %copy-start.7 = (s32[64]{0:T(128)S(1)}, s32[64]{0:T(128)}, u32[]{:S(2)}) copy-start(s32[64]{0:T(128)} %leaf_branch.1) | copy-start | bytes 772
  8.8 0.7 %copy-start.8 = (s32[4]{0:T(128)S(1)}, s32[4]{0:T(128)}, u32[]{:S(2)}) copy-start(s32[4]{0:T(128)} %branch_root.1) | copy-start | bytes 52
  9.5 0.7 %copy-start.9 = (s32[2]{0:T(128)S(1)}, s32[2]{0:T(128)}, u32[]{:S(2)}) copy-start(s32[2]{0:T(128)} %root_owner.1) | copy-start | bytes 28
  10.1 0.7 %copy-start.10 = (s32[4]{0:T(128)S(1)}, s32[4]{0:T(128)}, u32[]{:S(2)}) copy-start(s32[4]{0:T(128)} %branch_owner.1) | copy-start | bytes 52
  10.8 0.7 %copy-start.11 = (s32[2]{0:T(128)S(1)}, s32[2]{0:T(128)}, u32[]{:S(2)}) copy-start(s32[2]{0:T(128)} %root_len.1) | copy-start | bytes 28
  11.5 0.7 %copy-start.12 = (s32[4]{0:T(128)S(1)}, s32[4]{0:T(128)}, u32[]{:S(2)}) copy-start(s32[4]{0:T(128)} %branch_len.1) | copy-start | bytes 52
  12.1 0.7 %copy-start.13 = (s32[8]{0:T(128)S(1)}, s32[8]{0:T(128)}, u32[]{:S(2)}) copy-start(s32[8]{0:T(128)} %leaf_len.1) | copy-start | bytes 100
  12.8 0.7 %copy-start.14 = (f32[1,128]{1,0:T(1,128)S(1)}, f32[1,128]{1,0:T(1,128)}, u32[]{:S(2)}) copy-start(f32[1,128]{1,0:T(1,128)} %constant.2.clone.freq) | copy-start | bytes 1540

commit v2 on v1

--- a/solution.py
+++ b/solution.py
@@ -32,6 +32,22 @@
 def kernel(
     n,
     nt,
+    hidden_hbm,
+    gain_hbm,
+    freq_hbm,
+    leaf_branch_hbm,
+    branch_root_hbm,
+    root_owner_hbm,
+    branch_owner_hbm,
+    root_len_hbm,
+    branch_len_hbm,
+    leaf_len_hbm,
+    w_query,
+    w_keyval,
+    w_output,
+    node_hbm,
+    leaf_hbm,
+    result,
     hidden,
     gain,
     freq,
@@ -42,13 +58,6 @@
     root_len,
     branch_len,
     leaf_len,
-    w_query,
-    w_keyval,
-    w_output,
-    node_hbm,
-    leaf_hbm,
-    mixed,
-    entry,
     wq,
     wkv,
     wo,
@@ -86,6 +95,17 @@
         loads.append(copy)
         return copy
 
+    index_loads = [
+        load(leaf_branch_hbm, leaf_branch),
+        load(branch_root_hbm, branch_root),
+        load(root_len_hbm, root_len),
+        load(branch_len_hbm, branch_len),
+        load(leaf_len_hbm, leaf_len),
+        load(root_owner_hbm, root_owner),
+        load(branch_owner_hbm, branch_owner),
+        load(freq_hbm, freq),
+    ]
+    row_loads = [load(hidden_hbm, hidden), load(gain_hbm, gain)]
     q_loads = []
     for s in range(splits):
         part = pl.ds(s * depth, depth)
@@ -114,6 +134,8 @@
             barrier, inc=1, device_id=(lax.rem(mine + k, nt), me), device_id_type=MESH
         )
 
+    for copy in index_loads:
+        copy.wait()
     row8 = lax.broadcasted_iota(jnp.int32, (rows, LANES), 0)
     lane8 = lax.broadcasted_iota(jnp.int32, (rows, LANES), 1)
     low8 = lane8 < head_dim
@@ -141,6 +163,8 @@
         down = pltpu.roll(x, head_dim // 2, 1)
         return x * cosine + jnp.where(first_half, -up, down) * sine
 
+    for copy in row_loads:
+        copy.wait()
     widened = hidden[...].astype(F32)
     mean = jnp.sum(widened * widened, -1, keepdims=True) * (1.0 / width)
     normed = (widened * lax.rsqrt(mean + 1e-05) * gain[...]).astype(BF16)
@@ -172,7 +196,7 @@
     each(1, n, lambda k: q_copy(k).start())
 
     entry_new = jnp.where(low8, rotate(raw_entry), raw_entry).astype(BF16)
-    entry[...] = entry_new
+    result[:, cols:] = entry_new
     new32 = entry_new.astype(F32)
     swapped = pltpu.roll(new32, head_dim, 1)
     new_key = jnp.where(low8, new32, swapped)
@@ -340,7 +364,7 @@
         total = own_term[:, part]
         for k in range(1, nt):
             total = total + term_in[k].astype(F32)[c * rows : (c + 1) * rows]
-        mixed[:, part] = total.astype(BF16)
+        result[:, part] = total.astype(BF16)
 
     each(1, n, lambda k: q_copy(k).wait_send())
     each(1, n, lambda k: p_copy(k).wait_send())
@@ -375,41 +399,8 @@
     node = node_cache.reshape(-1, LANES)
     leaf = leaf_cache.reshape(-1, LANES)
     body_rows = inner // LANES * rows
-    vmem = pl.BlockSpec(memory_space=pltpu.VMEM)
-    smem = pl.BlockSpec(memory_space=pltpu.SMEM)
-    anywhere = pl.BlockSpec(memory_space=pl.ANY)
     dma = pltpu.SemaphoreType.DMA
-    mixed, entry = pl.pallas_call(
-        functools.partial(kernel, n, nt),
-        out_shape=(
-            jax.ShapeDtypeStruct((rows, cols), BF16),
-            jax.ShapeDtypeStruct((rows, LANES), BF16),
-        ),
-        in_specs=[vmem] * 3 + [smem] * 7 + [anywhere] * 5,
-        out_specs=(vmem, vmem),
-        scratch_shapes=[
-            pltpu.VMEM(w_query.shape, BF16),
-            pltpu.VMEM(w_keyval.shape, BF16),
-            pltpu.VMEM((nt, inner, cols), BF16),
-            pltpu.VMEM(node.shape, BF16),
-            pltpu.VMEM(leaf.shape, BF16),
-            pltpu.VMEM((n, body_rows, LANES), BF16),
-            pltpu.VMEM((n, body_rows + 2 * rows, LANES), BF16),
-            pltpu.VMEM((n, body_rows + 2 * rows, LANES), BF16),
-            pltpu.VMEM((nt, cols // LANES * rows, LANES), BF16),
-            pltpu.VMEM((nt, cols // LANES * rows, LANES), BF16),
-            dma((8 + 2 + nt,)),
-            dma((n,)),
-            dma((n,)),
-            dma((n,)),
-            dma((n,)),
-            dma((nt,)),
-            dma((nt,)),
-        ],
-        compiler_params=pltpu.CompilerParams(
-            collective_id=0, has_side_effects=True, vmem_limit_bytes=40 * 1024 * 1024
-        ),
-    )(
+    operands = (
         hidden,
         norm_gain[None, :],
         freq,
@@ -426,7 +417,37 @@
         node,
         leaf,
     )
-    return (mixed, entry[:, None, :])
+    result = pl.pallas_call(
+        functools.partial(kernel, n, nt),
+        out_shape=jax.ShapeDtypeStruct((rows, cols + LANES), BF16),
+        in_specs=[pl.BlockSpec(memory_space=pltpu.HBM)] * len(operands),
+        out_specs=pl.BlockSpec(memory_space=pltpu.VMEM),
+        scratch_shapes=[
+            *[pltpu.VMEM(a.shape, a.dtype) for a in operands[:3]],
+            *[pltpu.SMEM(a.shape, a.dtype) for a in operands[3:10]],
+            pltpu.VMEM(w_query.shape, BF16),
+            pltpu.VMEM(w_keyval.shape, BF16),
+            pltpu.VMEM((nt, inner, cols), BF16),
+            pltpu.VMEM(node.shape, BF16),
+            pltpu.VMEM(leaf.shape, BF16),
+            pltpu.VMEM((n, body_rows, LANES), BF16),
+            pltpu.VMEM((n, body_rows + 2 * rows, LANES), BF16),
+            pltpu.VMEM((n, body_rows + 2 * rows, LANES), BF16),
+            pltpu.VMEM((nt, cols // LANES * rows, LANES), BF16),
+            pltpu.VMEM((nt, cols // LANES * rows, LANES), BF16),
+            dma((10 + 8 + 2 + nt,)),
+            dma((n,)),
+            dma((n,)),
+            dma((n,)),
+            dma((n,)),
+            dma((nt,)),
+            dma((nt,)),
+        ],
+        compiler_params=pltpu.CompilerParams(
+            collective_id=0, has_side_effects=True, vmem_limit_bytes=63 * 1024 * 1024
+        ),
+    )(*operands)
+    return (result[:, :cols], result[:, None, cols:])
 
 
 def solution(mesh):

time: 36.2 us -> 23.3 us (0.64)
  local copies, waits for them, and re-layouts: 13.9 us -> 2.54 us
  Pallas kernels: 21.1 us -> 19.9 us
    unnamed x32 -> x0, local copies, waits for them, and re-layouts: 13.9 us -> none
    slice x0 -> x1, local copies, waits for them, and re-layouts: none -> 1.29 us  [local(): return (result[:, :cols], result[:, None, cols:])]
    broadcast_in_dim x0 -> x1, local copies, waits for them, and re-layouts: none -> 1.24 us  [local(): return (result[:, :cols], result[:, None, cols:])]
    pallas_call x1, Pallas kernels: 21.1 us -> 19.9 us  [local(): pl.pallas_call(functools.partial(kernel, n, nt), out_shape=jax.ShapeDtype...]
where the time goes in v2:
time: 23.3 us; the launch traced here: 23.1 us
  Pallas kernels  19.9 us (85%)
  local copies, waits for them, and re-layouts  2.54 us (11%)
  between operations  0.64 us (3%)
    pallas_call x1, Pallas kernels, local(): pl.pallas_call(functools.partial(kernel, n, nt), out_shape=jax.ShapeDtype...  19.9 us
    slice x1, local copies, waits for them, and re-layouts, local(): return (result[:, :cols], result[:, None, cols:])  1.29 us
    broadcast_in_dim x1, local copies, waits for them, and re-layouts, local(): return (result[:, :cols], result[:, None, cols:])  1.24 us

profile of v2, /device:TPU:0, one launch (start us, length us, event | category | flops | bytes accessed | tf_op | source)
XLA Modules:
  0.0 23.1 jit_solution(7252747064890657153)
XLA Ops:
  0.6 19.9 %shard_map.158 = bf16[8,640]{1,0:T(8,128)(2,1)} custom-call(bf16[8,2048]{1,0:T(8,128)(2,1)} %hidden_hbm.1, f32[1,2048]{1,0:T(1,128)} %bitcast.7, f32[1,128]{1,0:T(1,128)} %constant.2.clone.freq_hbm, s32[64]{0:T(128)} %leaf_branch_hbm.1, s32[4]{0:T(128)} %branch_root_hbm.1, s32[2]{0:T(128)} %root_owner_hbm.1, s32[4]{0:T(128)} %branch_owner_hbm.1, ...), custom_call_target="tpu_custom_call" | custom-call | tf_op jit(solution)/shard_map/pallas_call | solution.py:420
  20.6 1.2 %slice_bitcast_fusion = bf16[8,1,128]{2,0,1:T(8,128)(2,1)} fusion(bf16[8,640]{1,0:T(8,128)(2,1)} %shard_map.158), kind=kLoop, calls=%fused_computation | loop fusion | bytes 4096 | tf_op jit(solution)/shard_map/broadcast_in_dim | solution.py:450
  21.8 1.3 %slice.6 = bf16[8,512]{1,0:T(8,128)(2,1)} slice(bf16[8,640]{1,0:T(8,128)(2,1)} %shard_map.158), slice={[0:8], [0:512]} | slice | bytes 16384 | tf_op jit(solution)/shard_map/slice | solution.py:450

commit v3 on v2

--- a/solution.py
+++ b/solution.py
@@ -47,7 +47,8 @@
     w_output,
     node_hbm,
     leaf_hbm,
-    result,
+    mixed,
+    entry,
     hidden,
     gain,
     freq,
@@ -196,7 +197,7 @@
     each(1, n, lambda k: q_copy(k).start())
 
     entry_new = jnp.where(low8, rotate(raw_entry), raw_entry).astype(BF16)
-    result[:, cols:] = entry_new
+    entry[...] = entry_new
     new32 = entry_new.astype(F32)
     swapped = pltpu.roll(new32, head_dim, 1)
     new_key = jnp.where(low8, new32, swapped)
@@ -215,38 +216,6 @@
 
     leaf_load.wait()
     leaf_keys, leaf_values = split_rows(leaf[...])
-    per_leaf = leaf.shape[0] // rows
-    column = lax.broadcasted_iota(jnp.int32, (rows, leaf.shape[0]), 1)
-    start = lax.broadcasted_iota(jnp.int32, (rows, leaf.shape[0]), 0) * per_leaf
-    usable = (column >= start) & (column < start + lengths[:, :1])
-    q32 = queries.astype(F32)
-    leaf_stats = [jnp.zeros((rows, LANES), F32), jnp.zeros((rows, LANES), F32)]
-    leaf_sum = []
-    leaf_scores = [dot(queries, keys, NT) for keys in leaf_keys]
-    leaf_weights = [[], []]
-    fresh = []
-    for c in range(chunks):
-        part = slice(c * rows, (c + 1) * rows)
-        product = q32[part] * new_key
-        pair = []
-        for e in range(2):
-            score = jnp.sum(jnp.where(low8 if e == 0 else ~low8, product, 0.0), -1, keepdims=True)
-            scores = jnp.where(usable, leaf_scores[e][part], FLOOR)
-            peak = jnp.maximum(jnp.max(scores, -1, keepdims=True), score)
-            weights = jnp.exp(scores - peak).astype(BF16).astype(F32)
-            weight = jnp.exp(score - peak).astype(BF16).astype(F32)
-            total = jnp.sum(weights, -1, keepdims=True) + weight
-            leaf_weights[e].append(weights)
-            pair.append(weight)
-            here = lane8 == 2 * c + e
-            leaf_stats[0] = jnp.where(here, peak, leaf_stats[0])
-            leaf_stats[1] = jnp.where(here, total, leaf_stats[1])
-        fresh.append(jnp.where(low8, pair[0], pair[1]) * new_value)
-    leaf_sum = jnp.concatenate(fresh, 0)
-    for e in range(2):
-        leaf_sum = leaf_sum + dot(
-            jnp.concatenate(leaf_weights[e], 0).astype(BF16), leaf_values[e], NN
-        )
 
     block = min(n, 8)
 
@@ -307,6 +276,39 @@
             )
     each(1, n, lambda k: p_copy(k).start())
     part_in[0] = part_out[0]
+
+    per_leaf = leaf.shape[0] // rows
+    column = lax.broadcasted_iota(jnp.int32, (rows, leaf.shape[0]), 1)
+    start = lax.broadcasted_iota(jnp.int32, (rows, leaf.shape[0]), 0) * per_leaf
+    usable = (column >= start) & (column < start + lengths[:, :1])
+    q32 = queries.astype(F32)
+    leaf_stats = [jnp.zeros((rows, LANES), F32), jnp.zeros((rows, LANES), F32)]
+    leaf_scores = [dot(queries, keys, NT) for keys in leaf_keys]
+    leaf_weights = [[], []]
+    fresh = []
+    for c in range(chunks):
+        part = slice(c * rows, (c + 1) * rows)
+        product = q32[part] * new_key
+        pair = []
+        for e in range(2):
+            score = jnp.sum(jnp.where(low8 if e == 0 else ~low8, product, 0.0), -1, keepdims=True)
+            scores = jnp.where(usable, leaf_scores[e][part], FLOOR)
+            peak = jnp.maximum(jnp.max(scores, -1, keepdims=True), score)
+            weights = jnp.exp(scores - peak).astype(BF16).astype(F32)
+            weight = jnp.exp(score - peak).astype(BF16).astype(F32)
+            total = jnp.sum(weights, -1, keepdims=True) + weight
+            leaf_weights[e].append(weights)
+            pair.append(weight)
+            here = lane8 == 2 * c + e
+            leaf_stats[0] = jnp.where(here, peak, leaf_stats[0])
+            leaf_stats[1] = jnp.where(here, total, leaf_stats[1])
+        fresh.append(jnp.where(low8, pair[0], pair[1]) * new_value)
+    leaf_sum = jnp.concatenate(fresh, 0)
+    for e in range(2):
+        leaf_sum = leaf_sum + dot(
+            jnp.concatenate(leaf_weights[e], 0).astype(BF16), leaf_values[e], NN
+        )
+
     each(1, n, lambda k: p_copy(k).wait_recv())
 
     row_of = lax.rem(lax.broadcasted_iota(jnp.int32, part_in.shape[1:], 0), rows)
@@ -364,12 +366,21 @@
         total = own_term[:, part]
         for k in range(1, nt):
             total = total + term_in[k].astype(F32)[c * rows : (c + 1) * rows]
-        result[:, part] = total.astype(BF16)
+        mixed[:, part] = total.astype(BF16)
 
     each(1, n, lambda k: q_copy(k).wait_send())
     each(1, n, lambda k: p_copy(k).wait_send())
     for k in range(1, nt):
         t_copy(k).wait_send()
+
+
+def deliver(mixed, entry, mixed_out, entry_out, sem):
+    first = pltpu.make_async_copy(mixed, mixed_out, sem.at[0])
+    second = pltpu.make_async_copy(entry, entry_out, sem.at[1])
+    first.start()
+    second.start()
+    first.wait()
+    second.wait()
 
 
 def local(
@@ -400,6 +411,10 @@
     leaf = leaf_cache.reshape(-1, LANES)
     body_rows = inner // LANES * rows
     dma = pltpu.SemaphoreType.DMA
+    shapes = (
+        jax.ShapeDtypeStruct((rows, cols), BF16),
+        jax.ShapeDtypeStruct((rows, LANES), BF16),
+    )
     operands = (
         hidden,
         norm_gain[None, :],
@@ -417,11 +432,11 @@
         node,
         leaf,
     )
-    result = pl.pallas_call(
+    mixed, entry = pl.pallas_call(
         functools.partial(kernel, n, nt),
-        out_shape=jax.ShapeDtypeStruct((rows, cols + LANES), BF16),
+        out_shape=shapes,
         in_specs=[pl.BlockSpec(memory_space=pltpu.HBM)] * len(operands),
-        out_specs=pl.BlockSpec(memory_space=pltpu.VMEM),
+        out_specs=(pl.BlockSpec(memory_space=pltpu.VMEM),) * 2,
         scratch_shapes=[
             *[pltpu.VMEM(a.shape, a.dtype) for a in operands[:3]],
             *[pltpu.SMEM(a.shape, a.dtype) for a in operands[3:10]],
@@ -447,7 +462,16 @@
             collective_id=0, has_side_effects=True, vmem_limit_bytes=63 * 1024 * 1024
         ),
     )(*operands)
-    return (result[:, :cols], result[:, None, cols:])
+    anywhere = pl.BlockSpec(memory_space=pl.ANY)
+    mixed, entry = pl.pallas_call(
+        deliver,
+        out_shape=shapes,
+        in_specs=[anywhere] * 2,
+        out_specs=(anywhere,) * 2,
+        scratch_shapes=[dma((2,))],
+        compiler_params=pltpu.CompilerParams(vmem_limit_bytes=63 * 1024 * 1024),
+    )(mixed, entry)
+    return (mixed, entry[:, None, :])
 
 
 def solution(mesh):

time: 23.3 us -> 22.4 us (0.961)
  local copies, waits for them, and re-layouts: 2.54 us -> 0 us
  Pallas kernels: 19.9 us -> 21.6 us
    pallas_call x1 -> x2, Pallas kernels: 19.9 us -> 21.6 us  [the longest x1 20.2 us: local(): pl.pallas_call(functools.partial(kernel, n, nt), out_shape=shapes, in_spe...]
    slice x1 -> x0, local copies, waits for them, and re-layouts: 1.29 us -> none  [local(): return (result[:, :cols], result[:, None, cols:])]
    broadcast_in_dim x1 -> x0, local copies, waits for them, and re-layouts: 1.24 us -> none  [local(): return (result[:, :cols], result[:, None, cols:])]
where the time goes in v3:
time: 22.4 us; the launch traced here: 22.3 us
  Pallas kernels  21.6 us (96%)
  between operations  0.64 us (3%)
    pallas_call x1, Pallas kernels, local(): pl.pallas_call(functools.partial(kernel, n, nt), out_shape=shapes, in_spe...  20.2 us
    pallas_call x1, Pallas kernels, local(): pl.pallas_call(deliver, out_shape=shapes, in_specs=[anywhere] * 2, out_sp...  1.43 us

profile of v3, /device:TPU:0, one launch (start us, length us, event | category | flops | bytes accessed | tf_op | source)
XLA Modules:
  0.0 22.3 jit_solution(15587987274459943084)
XLA Ops:
  0.6 20.2 %shard_map.158 = (bf16[8,512]{1,0:T(8,128)(2,1)}, bf16[8,128]{1,0:T(8,128)(2,1)}) custom-call(bf16[8,2048]{1,0:T(8,128)(2,1)} %hidden_hbm.1, f32[1,2048]{1,0:T(1,128)} %bitcast.6, f32[1,128]{1,0:T(1,128)} %constant.2.clone.freq_hbm, s32[64]{0:T(128)} %leaf_branch_hbm.1, s32[4]{0:T(128)} %branch_root_hbm.1, s32[2]{0:T(128)} %root_owner_hbm.1, ...), custom_call_target="tpu_custom_call" | custom-call | tf_op jit(solution)/shard_map/pallas_call | solution.py:435
  20.9 1.4 %shard_map.159 = (bf16[8,512]{1,0:T(8,128)(2,1)}, bf16[8,128]{1,0:T(8,128)(2,1)}) custom-call(bf16[8,512]{1,0:T(8,128)(2,1)} %get-tuple-element.6.mixed, bf16[8,128]{1,0:T(8,128)(2,1)} %get-tuple-element.7.entry), custom_call_target="tpu_custom_call" | custom-call | tf_op jit(solution)/shard_map/pallas_call | solution.py:466

commit v4 on v3

--- a/solution.py
+++ b/solution.py
@@ -115,12 +115,6 @@
         )
     node_load = load(node_hbm, node)
     leaf_load = load(leaf_hbm, leaf)
-    o_loads = []
-    for k in range(nt):
-        target = lax.rem(mine + k, nt)
-        o_loads.append(
-            load(w_output.at[:, pl.ds(pl.multiple_of(target * cols, cols), cols)], wo.at[k])
-        )
 
     barrier = pltpu.get_barrier_semaphore()
 
@@ -196,6 +190,13 @@
 
     each(1, n, lambda k: q_copy(k).start())
 
+    o_loads = []
+    for k in range(nt):
+        target = lax.rem(mine + k, nt)
+        o_loads.append(
+            load(w_output.at[:, pl.ds(pl.multiple_of(target * cols, cols), cols)], wo.at[k])
+        )
+
     entry_new = jnp.where(low8, rotate(raw_entry), raw_entry).astype(BF16)
     entry[...] = entry_new
     new32 = entry_new.astype(F32)
@@ -217,7 +218,7 @@
     leaf_load.wait()
     leaf_keys, leaf_values = split_rows(leaf[...])
 
-    block = min(n, 8)
+    block = 4 if n == 8 else min(n, 8)
 
     def p_copy(k):
         return pltpu.make_async_remote_copy(
@@ -263,18 +264,17 @@
                 0,
             ).astype(BF16)
 
-    each(1, n, lambda k: q_copy(k).wait_recv())
-    for first in range(0, n, block):
-        if n == block:
-            owner_block(0)
-        elif first == 0:
-            lax.fori_loop(
-                0,
-                n // block,
-                lambda i, carry: (owner_block(i * block), carry)[1],
-                0,
-            )
-    each(1, n, lambda k: p_copy(k).start())
+    if n <= 2 * block:
+        for first in range(0, n, block):
+            each(max(first, 1), first + block, lambda k: q_copy(k).wait_recv())
+            owner_block(first)
+            each(max(first, 1), first + block, lambda k: p_copy(k).start())
+    else:
+        each(1, n, lambda k: q_copy(k).wait_recv())
+        lax.fori_loop(
+            0, n // block, lambda i, carry: (owner_block(i * block), carry)[1], 0
+        )
+        each(1, n, lambda k: p_copy(k).start())
     part_in[0] = part_out[0]
 
     per_leaf = leaf.shape[0] // rows

time: 22.4 us -> 21.7 us (0.969)
  Pallas kernels: 21.6 us -> 20.9 us
    pallas_call x1, Pallas kernels: 20.2 us -> 19.4 us  [local(): pl.pallas_call(functools.partial(kernel, n, nt), out_shape=shapes, in_spe...]
where the time goes in v4:
time: 21.7 us; the launch traced here: 21.5 us
  Pallas kernels  20.9 us (96%)
  between operations  0.64 us (3%)
    pallas_call x1, Pallas kernels, local(): pl.pallas_call(functools.partial(kernel, n, nt), out_shape=shapes, in_spe...  19.4 us
    pallas_call x1, Pallas kernels, local(): pl.pallas_call(deliver, out_shape=shapes, in_specs=[anywhere] * 2, out_sp...  1.43 us

profile of v4, /device:TPU:0, one launch (start us, length us, event | category | flops | bytes accessed | tf_op | source)
XLA Modules:
  0.0 21.5 jit_solution(11792394454883431766)
XLA Ops:
  0.6 19.4 %shard_map.158 = (bf16[8,512]{1,0:T(8,128)(2,1)}, bf16[8,128]{1,0:T(8,128)(2,1)}) custom-call(bf16[8,2048]{1,0:T(8,128)(2,1)} %hidden_hbm.1, f32[1,2048]{1,0:T(1,128)} %bitcast.6, f32[1,128]{1,0:T(1,128)} %constant.2.clone.freq_hbm, s32[64]{0:T(128)} %leaf_branch_hbm.1, s32[4]{0:T(128)} %branch_root_hbm.1, s32[2]{0:T(128)} %root_owner_hbm.1, ...), custom_call_target="tpu_custom_call" | custom-call | tf_op jit(solution)/shard_map/pallas_call | solution.py:435
  20.1 1.4 %shard_map.159 = (bf16[8,512]{1,0:T(8,128)(2,1)}, bf16[8,128]{1,0:T(8,128)(2,1)}) custom-call(bf16[8,512]{1,0:T(8,128)(2,1)} %get-tuple-element.6.mixed, bf16[8,128]{1,0:T(8,128)(2,1)} %get-tuple-element.7.entry), custom_call_target="tpu_custom_call" | custom-call | tf_op jit(solution)/shard_map/pallas_call | solution.py:466

commit v5 on v4

--- a/solution.py
+++ b/solution.py
@@ -110,9 +110,8 @@
     q_loads = []
     for s in range(splits):
         part = pl.ds(s * depth, depth)
-        q_loads.append(
-            (load(w_query.at[part], wq.at[part]), load(w_keyval.at[part], wkv.at[part]))
-        )
+        q_loads.append(load(w_query.at[part], wq.at[part]))
+    entry_load = load(w_keyval, wkv)
     node_load = load(node_hbm, node)
     leaf_load = load(leaf_hbm, leaf)
 
@@ -164,13 +163,10 @@
     mean = jnp.sum(widened * widened, -1, keepdims=True) * (1.0 / width)
     normed = (widened * lax.rsqrt(mean + 1e-05) * gain[...]).astype(BF16)
     raw = jnp.zeros((rows, wq.shape[1]), F32)
-    raw_entry = jnp.zeros((rows, LANES), F32)
     for s in range(splits):
-        for copy in q_loads[s]:
-            copy.wait()
+        q_loads[s].wait()
         part = slice(s * depth, (s + 1) * depth)
         raw = raw + dot(normed[:, part], wq[part, :], NN)
-        raw_entry = raw_entry + dot(normed[:, part], wkv[part, :], NN)
     queries = jnp.concatenate(
         [rotate(raw[:, c * LANES : (c + 1) * LANES]) * factor for c in range(chunks)], 0
     ).astype(BF16)
@@ -197,6 +193,8 @@
             load(w_output.at[:, pl.ds(pl.multiple_of(target * cols, cols), cols)], wo.at[k])
         )
 
+    entry_load.wait()
+    raw_entry = dot(normed, wkv[...], NN)
     entry_new = jnp.where(low8, rotate(raw_entry), raw_entry).astype(BF16)
     entry[...] = entry_new
     new32 = entry_new.astype(F32)

time: 21.7 us -> 21.6 us (level)
  no operation moved by 1% of the time
where the time goes in v5:
time: 21.6 us; the launch traced here: 21.5 us
  Pallas kernels  20.8 us (96%)
  between operations  0.64 us (3%)
    pallas_call x1, Pallas kernels, local(): pl.pallas_call(functools.partial(kernel, n, nt), out_shape=shapes, in_spe...  19.4 us
    pallas_call x1, Pallas kernels, local(): pl.pallas_call(deliver, out_shape=shapes, in_specs=[anywhere] * 2, out_sp...  1.43 us

profile of v5, /device:TPU:0, one launch (start us, length us, event | category | flops | bytes accessed | tf_op | source)
XLA Modules:
  0.0 21.5 jit_solution(7212960891208583931)
XLA Ops:
  0.6 19.4 %shard_map.158 = (bf16[8,512]{1,0:T(8,128)(2,1)}, bf16[8,128]{1,0:T(8,128)(2,1)}) custom-call(bf16[8,2048]{1,0:T(8,128)(2,1)} %hidden_hbm.1, f32[1,2048]{1,0:T(1,128)} %bitcast.6, f32[1,128]{1,0:T(1,128)} %constant.2.clone.freq_hbm, s32[64]{0:T(128)} %leaf_branch_hbm.1, s32[4]{0:T(128)} %branch_root_hbm.1, s32[2]{0:T(128)} %root_owner_hbm.1, ...), custom_call_target="tpu_custom_call" | custom-call | tf_op jit(solution)/shard_map/pallas_call | solution.py:433
  20.1 1.4 %shard_map.159 = (bf16[8,512]{1,0:T(8,128)(2,1)}, bf16[8,128]{1,0:T(8,128)(2,1)}) custom-call(bf16[8,512]{1,0:T(8,128)(2,1)} %get-tuple-element.6.mixed, bf16[8,128]{1,0:T(8,128)(2,1)} %get-tuple-element.7.entry), custom_call_target="tpu_custom_call" | custom-call | tf_op jit(solution)/shard_map/pallas_call | solution.py:464
